TPU v7x, 512 devices: a whole 4x8x8 slice. The times are simulated.
512 devices in a mesh: expert: 32 (over x, z), row: 16 (over y, core).
Axes of the slice: x: 4, y: 8, z: 8, core: 2. Of those that a mesh axis runs over, the one named last changes fastest.
Arguments:
- momentum: bfloat16 [32, 3584, 2048], P('expert', 'row'), may hold values from -6 to 6
- gradient: bfloat16 [32, 3584, 2048], P('expert', 'row'), may hold values from -96 to 96
- basis: float32 [32, 2048, 512], P('expert', 'row'), may hold values from -0.125 to 0.125
- ranks: int32 [32], replicated, may hold values from 128 to 512, as said below
- assignment: int32 [32], replicated, may hold values from 0 to 31, each once
Outputs:
- new_momentum: bfloat16 [32, 3584, 2048], P('expert', 'row')
- update: bfloat16 [32, 3584, 2048], P('expert', 'row')
- new_basis: float32 [32, 2048, 512], P('expert', 'row')
Inputs may be any that keep to these rules, and one draw needn't show every extreme that they name: `ranks`: some expert has rank 512 in every draw.
All inputs are finite; a program needn't handle non-finite values.
Results may differ from a plain program's by a relative error of at most 0.033.
Values may be sent and summed in bfloat16 or wider, within the bound.
A program may use at most 64 MiB of HBM per device.

v0:
```python
import math

import jax
import jax.numpy as jnp
from jax import lax
from jax.sharding import Mesh
from jax.sharding import PartitionSpec as P

ROWS = 3584
FF = 2048
RANK_MAX = 512
EXPERT_ROW = ("expert_0", "expert_1", "row_0", "row_1")
ROW = ("row_0", "row_1")
EXPERT = ("expert_0", "expert_1")


epsilon = 1e-06
mu_decay = 0.9
clip_target = 0.5


def by_axis(value, axes):
    for axis in axes:
        value = lax.psum(value, axis)
    return value


def gathered_by_axis(value, axes, dim):
    if not axes:
        return value
    nearer = lax.all_gather(value, axes[-1], axis=dim, tiled=True)
    return gathered_by_axis(nearer, axes[:-1], dim)


def padded_to(lines, size):
    spare = -len(lines) % size
    return jnp.pad(lines, [(0, spare)] + [(0, 0)] * (lines.ndim - 1))


def reduced_to_own(pieces, axes, turns):
    dims = [lax.axis_size(a) for a in axes]
    pieces = pieces.reshape(*dims, *pieces.shape[1:])
    pieces = pieces.transpose(*turns, *range(len(axes), pieces.ndim))
    pieces = pieces.reshape(-1, *pieces.shape[len(axes) :])
    for k in turns:
        pieces = lax.psum_scatter(pieces, axes[k], scatter_dimension=0, tiled=True)
    return pieces[0]


def all_blocks(value, axes, turns):
    pieces = value[None]
    for k in turns:
        pieces = lax.all_gather(pieces, axes[k], axis=0, tiled=True)
    carried = [lax.axis_size(axes[k]) for k in reversed(turns)]
    pieces = pieces.reshape(*carried, *value.shape)
    turned = sorted(range(len(turns)), key=lambda place: turns[len(turns) - 1 - place])
    return pieces.transpose(*turned, *range(len(turns), pieces.ndim)).reshape(-1, *value.shape)


def total_of(value, axes, turns):
    size, lines = (lax.axis_size(axes), value.reshape(-1, *value.shape[1:][-1:]))
    pieces = padded_to(lines, size).reshape(size, -1, *lines.shape[1:])
    own = reduced_to_own(pieces, axes, turns)
    whole = all_blocks(own, axes, turns[::-1]).reshape(-1, *lines.shape[1:])
    return whole[: len(lines)].reshape(value.shape)


def local(momentum, gradient, basis, ranks, assignment):
    grad_full = gradient[0].astype(jnp.float32)
    total_sq = by_axis(jnp.sum(grad_full * grad_full), EXPERT_ROW)
    entry_count = float(
        gradient.shape[1] * gradient.shape[2] * lax.axis_size(ROW) * lax.axis_size(EXPERT)
    )
    clip_scale = jnp.minimum(1.0, clip_target * lax.rsqrt(total_sq / entry_count + epsilon))
    buffer_full = momentum[0].astype(jnp.float32) + clip_scale * grad_full
    buffer = buffer_full.astype(jnp.bfloat16)
    group_index = lax.axis_index(EXPERT)
    slot_ids = jnp.arange(assignment.shape[0], dtype=jnp.int32)
    expert_id = jnp.sum(jnp.where(slot_ids == group_index, assignment, 0))
    rank_now = jnp.sum(jnp.where(slot_ids == expert_id, ranks, 0))
    width = basis.shape[2]
    keep_mask = (jnp.arange(width, dtype=jnp.int32) < rank_now).astype(jnp.float32)
    basis_half = (basis[0] * keep_mask[None, :]).astype(jnp.bfloat16)
    power_cols = jnp.dot(
        buffer, gathered_by_axis(basis_half, ROW, 0), preferred_element_type=jnp.float32
    )
    gram_part = lax.dot_general(
        power_cols, power_cols, (((0,), (0,)), ((), ())), preferred_element_type=jnp.float32
    )
    gram_sum = total_of(gram_part.astype(jnp.bfloat16), ROW, (0, 1)).astype(jnp.float32)
    gram_sum = gram_sum * keep_mask[:, None] * keep_mask[None, :] + jnp.diag(1.0 - keep_mask)
    lower_factor = jnp.linalg.cholesky(gram_sum)
    identity = jnp.eye(width, dtype=jnp.float32)
    inverse = lax.linalg.triangular_solve(lower_factor, identity, left_side=True, lower=True)
    orthonormal = lax.dot_general(
        power_cols, inverse, (((1,), (1,)), ((), ())), preferred_element_type=jnp.float32
    )
    ortho_half = orthonormal.astype(jnp.bfloat16)
    buffer_cols = lax.all_to_all(buffer, ROW, split_axis=1, concat_axis=0, tiled=True)
    factor = lax.dot_general(
        buffer_cols,
        lax.all_gather(ortho_half, ROW, axis=0, tiled=True),
        (((0,), (0,)), ((), ())),
        preferred_element_type=jnp.float32,
    )
    factor_whole = lax.all_gather(factor.astype(jnp.bfloat16), ROW, axis=0, tiled=True).astype(
        factor.dtype
    )
    col_sq = jnp.sum(factor_whole * factor_whole, axis=0)
    factor_half = factor_whole.astype(jnp.bfloat16)
    inv_norm = lax.rsqrt(col_sq + epsilon)
    new_basis = factor * inv_norm[None, :]
    feedback = lax.dot_general(
        ortho_half, factor_half, (((1,), (1,)), ((), ())), preferred_element_type=jnp.float32
    )
    new_momentum = (buffer_full - (1.0 - mu_decay) * feedback).astype(jnp.bfloat16)
    update_gain = math.sqrt(ROWS * FF / RANK_MAX)
    scaled = (orthonormal * (inv_norm * update_gain)[None, :]).astype(jnp.bfloat16)
    update = lax.dot_general(
        scaled, factor_half, (((1,), (1,)), ((), ())), preferred_element_type=jnp.float32
    ).astype(jnp.bfloat16)
    return (new_momentum[None], update[None], new_basis[None])


def solution(mesh):
    torus = Mesh(mesh.devices.reshape(4, 8, 8, 2), ("expert_0", "expert_1", "row_0", "row_1"))
    return jax.shard_map(
        local,
        mesh=torus,
        in_specs=(P(EXPERT, ROW, None), P(EXPERT, ROW, None), P(EXPERT, ROW, None), P(), P()),
        out_specs=(P(EXPERT, ROW, None), P(EXPERT, ROW, None), P(EXPERT, ROW, None)),
        check_vma=False,
    )
```

profile of v0, /device:TPU:1, one launch (start us, length us, event | category | flops | bytes accessed | tf_op | source)
XLA Modules:
  0.0 423.0 jit_solution(11498126879111925834)
XLA Ops:
  8.7 1.9 fusion.51
  12.2 8.6 %all_gather.18 = bf16[256,512]{1,0:T(8,128)(2,1)} all-gather(bf16[128,512]{1,0:T(8,128)(2,1)S(1)} %fusion.29), channel_id=1, replica_groups=mesh['expert_0'=4,'expert_1'=8,'row_0'=8,'row_1'=2] {'row_1'}, dimensions={0}, use_global_device_ids=true | all-gather | bytes 393216 | tf_op jit(solution)/shard_map/all_gather | solution.py:31
  20.9 2.3 fusion.4
  23.2 6.7 %psum.28 = f32[]{:T(128)} all-reduce(f32[]{:T(128)} %fusion.4), channel_id=1, replica_groups=mesh['expert_0'=4,'expert_1'=8,'row_0'=8,'row_1'=2] {'expert_0'}, use_global_device_ids=true, to_apply=%region_1.0 | all-reduce | flops 1 | bytes 8 | tf_op jit(solution)/shard_map/psum | solution.py:24
  29.9 18.0 %psum.29 = f32[]{:T(128)} all-reduce(f32[]{:T(128)} %psum.28), channel_id=1, replica_groups=mesh['expert_0'=4,'expert_1'=8,'row_0'=8,'row_1'=2] {'expert_1'}, use_global_device_ids=true, to_apply=%region_2.0 | all-reduce | flops 1 | bytes 8 | tf_op jit(solution)/shard_map/psum | solution.py:24
  48.0 15.5 %psum.30 = f32[]{:T(128)} all-reduce(f32[]{:T(128)} %psum.29), channel_id=1, replica_groups=mesh['expert_0'=4,'expert_1'=8,'row_0'=8,'row_1'=2] {'row_0'}, use_global_device_ids=true, to_apply=%region_3.0 | all-reduce | flops 1 | bytes 8 | tf_op jit(solution)/shard_map/psum | solution.py:24
  63.5 10.6 %psum.31 = f32[]{:T(128)} all-reduce(f32[]{:T(128)} %psum.30), channel_id=1, replica_groups=mesh['expert_0'=4,'expert_1'=8,'row_0'=8,'row_1'=2] {'row_1'}, use_global_device_ids=true, to_apply=%region_4.0 | all-reduce | flops 1 | bytes 8 | tf_op jit(solution)/shard_map/psum | solution.py:24
  74.8 2.2 fusion.17
  79.0 25.8 %reduce-scatter.3.cloned.1.call-done = bf16[2,32,512]{2,1,0:T(8,128)(2,1)} async-done(((bf16[16,32,512]{2,1,0:T(8,128)(2,1)}), bf16[2,32,512]{2,1,0:T(8,128)(2,1)}) %reduce-scatter.3.cloned.1.call-update) | async-done | bytes 65552 | tf_op jit(solution)/shard_map/reduce_scatter | solution.py:46
  106.0 22.8 %reduce-scatter.5.cloned.1.call-done = bf16[1,32,512]{2,1,0:T(8,128)(2,1)} async-done(((bf16[2,32,512]{2,1,0:T(8,128)(2,1)}), bf16[1,32,512]{2,1,0:T(8,128)(2,1)}) %reduce-scatter.5.cloned.1.call-update) | async-done | bytes 32784 | tf_op jit(solution)/shard_map/reduce_scatter | solution.py:46
  128.9 2.1 all_gather.20
  130.9 19.9 %all_gather.21 = bf16[16,32,512]{2,1,0:T(8,128)(2,1)S(1)} all-gather(bf16[2,32,512]{2,1,0:T(8,128)(2,1)S(1)} %all_gather.20), channel_id=1, replica_groups=mesh['expert_0'=4,'expert_1'=8,'row_0'=8,'row_1'=2] {'row_0'}, dimensions={0}, use_global_device_ids=true | all-gather | bytes 589824 | tf_op jit(solution)/shard_map/all_gather | solution.py:53
  154.3 11.7 %cholesky.103 = f32[128,128]{1,0:T(8,128)S(1)} custom-call(f32[128,128]{1,0:T(8,128)S(1)} %cholesky.263), custom_call_target="Cholesky" | custom-call | tf_op jit(solution)/shard_map/jit(cholesky)/cholesky | solution.py:92
  166.1 9.8 %custom-call.30 = f32[1,128,128]{1,2,0:T(8,128)S(1)} custom-call(f32[1,128,128]{2,1,0:T(8,128)S(1)} %get-tuple-element.38), custom_call_target="InvertDiagBlocksLowerTriangular" | custom-call | tf_op jit(solution)/shard_map/jit(cholesky)/cholesky | solution.py:92
  176.8 11.7 %cholesky.215 = f32[128,128]{1,0:T(8,128)S(1)} custom-call(f32[128,128]{1,0:T(8,128)S(1)} %cholesky.267), custom_call_target="Cholesky" | custom-call | tf_op jit(solution)/shard_map/jit(cholesky)/cholesky | solution.py:92
  188.6 10.0 %custom-call.31 = f32[1,128,128]{1,2,0:T(8,128)S(1)} custom-call(f32[1,128,128]{2,1,0:T(8,128)S(1)} %get-tuple-element.36), custom_call_target="InvertDiagBlocksLowerTriangular" | custom-call | tf_op jit(solution)/shard_map/jit(cholesky)/cholesky | solution.py:92
  200.6 11.7 %cholesky.236 = f32[128,128]{1,0:T(8,128)S(1)} custom-call(f32[128,128]{1,0:T(8,128)S(1)} %cholesky.272), custom_call_target="Cholesky" | custom-call | tf_op jit(solution)/shard_map/jit(cholesky)/cholesky | solution.py:92
  212.4 9.8 %custom-call.32 = f32[1,128,128]{1,2,0:T(8,128)S(1)} custom-call(f32[1,128,128]{2,1,0:T(8,128)S(1)} %get-tuple-element.34), custom_call_target="InvertDiagBlocksLowerTriangular" | custom-call | tf_op jit(solution)/shard_map/jit(cholesky)/cholesky | solution.py:92
  223.9 11.9 %cholesky.253 = f32[128,128]{1,0:T(8,128)S(1)} custom-call(f32[128,128]{1,0:T(8,128)S(1)} %convolution_subtract_fusion.5), custom_call_target="Cholesky" | custom-call | tf_op jit(solution)/shard_map/jit(cholesky)/cholesky | solution.py:92
  241.7 14.4 %while.1 = (s32[]{:T(128)}, f32[512,512]{0,1:T(8,128)}, s32[4,2]{0,1:T(2,128)S(1)}, f32[4,128,128]{2,1,0:T(8,128)}, s32[]{:T(128)}) while((s32[]{:T(128)}, f32[512,512]{0,1:T(8,128)}, s32[4,2]{0,1:T(2,128)S(1)}, f32[4,128,128]{2,1,0:T(8,128)}, s32[]{:T(128)}) %tuple.33), condition=%wide.while_cond, body=%wide.while_body.sunk | while | flops 2 | bytes 393329 | solution.py:94
  242.3 2.3 dynamic-slice.7
  245.9 2.3 dynamic-slice.7
  249.5 2.3 dynamic-slice.7
  253.1 2.2 dynamic-slice.7
  256.1 40.1 %custom-call.33 = f32[4,128,128]{1,2,0:T(8,128)S(1)} custom-call(f32[4,128,128]{2,1,0:T(8,128)} %get-tuple-element.10), custom_call_target="InvertDiagBlocksLowerTriangular" | custom-call | tf_op jit(solution)/shard_map/triangular_solve | solution.py:94
  298.4 1.9 convolution_subtract_fusion
  300.8 2.4 convolution_subtract_fusion.2
  305.6 43.9 %all_to_all.16 = bf16[224,16,128]{2,0,1:T(8,128)(2,1)S(1)} all-to-all(bf16[224,16,128]{2,0,1:T(8,128)(2,1)S(1)} %copy.42), channel_id=1, replica_groups=mesh['expert_0'=4,'expert_1'=8,'row_0'=8,'row_1'=2] {'row_0','row_1'}, dimensions={1} | all-to-all | bytes 1835008 | tf_op jit(solution)/shard_map/all_to_all | solution.py:99
  349.6 15.3 %all-gather.6.cloned.1.call-done = bf16[3584,512]{1,0:T(8,128)(2,1)} async-done(((bf16[224,512]{1,0:T(8,128)(2,1)}), bf16[3584,512]{1,0:T(8,128)(2,1)}) %all-gather.6.cloned.1.call-update) | async-done | bytes 3670032 | tf_op jit(solution)/shard_map/all_gather | solution.py:102
  364.8 3.4 fusion.57
  368.2 41.6 %all-gather.8.cloned.1.call-done = bf16[2048,512]{1,0:T(8,128)(2,1)} async-done(((bf16[128,512]{1,0:T(8,128)(2,1)}), bf16[2048,512]{1,0:T(8,128)(2,1)}) %all-gather.8.cloned.1.call-update) | async-done | bytes 2097168 | tf_op jit(solution)/shard_map/all_gather | solution.py:106
  409.8 2.2 multiply_reduce_fusion
  (98 shorter events, 32.3 us)
Async XLA Ops:
  7.2 67.6 %copy-start.1 = (bf16[1,224,2048]{2,1,0:T(8,128)(2,1)S(1)}, bf16[1,224,2048]{2,1,0:T(8,128)(2,1)}, u32[]{:S(2)}) copy-start(bf16[1,224,2048]{2,1,0:T(8,128)(2,1)} %param.6) | copy-start | bytes 2752516
  7.2 67.6 %copy-start.2 = (bf16[1,224,2048]{2,1,0:T(8,128)(2,1)S(1)}, bf16[1,224,2048]{2,1,0:T(8,128)(2,1)}, u32[]{:S(2)}) copy-start(bf16[1,224,2048]{2,1,0:T(8,128)(2,1)} %param.5) | copy-start | bytes 2752516
  7.2 67.6 %all-gather.4.cloned.1.call-start = ((), (), s32[]{:S(2)}) async-start(), calls=%async_computation.3 | async-start | bytes 2359296 | tf_op jit(solution)/shard_map/all_gather | solution.py:31
  20.9 84.0 %reduce-scatter.3.cloned.1.call-start = ((), (), s32[]{:S(2)}) async-start(), calls=%async_computation.4 | async-start | bytes 589824 | tf_op jit(solution)/shard_map/reduce_scatter | solution.py:46
  78.2 50.7 %reduce-scatter.5.cloned.1.call-start = ((), (), s32[]{:S(2)}) async-start(), calls=%async_computation.5 | async-start | bytes 98304 | tf_op jit(solution)/shard_map/reduce_scatter | solution.py:46
  104.9 259.9 %all-gather.6.cloned.1.call-start = ((), (), s32[]{:S(2)}) async-start(), calls=%async_computation.6 | async-start | bytes 3899392 | tf_op jit(solution)/shard_map/all_gather | solution.py:102
  154.3 34.4 %copy-start.5 = (f32[512,512]{1,0:T(8,128)}, f32[512,512]{1,0:T(8,128)S(1)}, u32[]{:S(2)}) copy-start(f32[512,512]{1,0:T(8,128)S(1)} %fusion.15) | copy-start | bytes 3145732
  240.5 56.1 %copy-start.4 = (f32[512,512]{0,1:T(8,128)S(1)}, f32[512,512]{0,1:T(8,128)}, u32[]{:S(2)}) copy-start(f32[512,512]{0,1:T(8,128)} %fusion.24) | copy-start | bytes 3145732
  303.2 1.7 copy-start.3
  304.8 105.0 %all-gather.8.cloned.1.call-start = ((), (), s32[]{:S(2)}) async-start(), calls=%async_computation.7 | async-start | bytes 2228224 | tf_op jit(solution)/shard_map/all_gather | solution.py:106
  368.2 44.6 %copy-start.6 = (bf16[224,512]{1,0:T(8,128)(2,1)S(1)}, bf16[224,512]{1,0:T(8,128)(2,1)}, u32[]{:S(2)}) copy-start(bf16[224,512]{1,0:T(8,128)(2,1)} %get-tuple-element.41) | copy-start | bytes 688132
  409.8 3.0 copy-start
  412.8 1.7 copy-start.7
Sparse Core Ops, SparseCore 0:
  21.0 38.9 all-gather.3
  78.3 26.4 reduce-scatter.2
  107.8 20.9 reduce-scatter.4
  304.9 59.8 all-gather.5
  368.3 41.4 all-gather.7
where the time goes:
time: 426 us; the launch traced here: 423 us
  other arithmetic  134 us (31%)
  blocking collectives  125 us (29%)
  waiting for transfers between devices  106 us (25%)
  matrix products  22.8 us (5%)
  between operations  17.7 us (4%)
  local copies, waits for them, and re-layouts  17.2 us (4%)
    another operation x14, other arithmetic, local(): lower_factor = jnp.linalg.cholesky(gram_sum)  78.7 us
    psum x4, blocking collectives, by_axis(): value = lax.psum(value, axis)  50.9 us
    reduce_scatter x2, waiting for transfers between devices, reduced_to_own(): pieces = lax.psum_scatter(pieces, axes[k], scatter_dimension=0, tiled=True)  48.7 us
    all_to_all x1, blocking collectives, local(): lax.all_to_all(buffer, ROW, split_axis=1, concat_axis=0, tiled=True)  43.9 us
    all_gather x1, waiting for transfers between devices, local(): lax.all_gather(factor.astype(jnp.bfloat16), ROW, axis=0, tiled=True)  41.6 us
    another operation x3, other arithmetic, local(): lax.linalg.triangular_solve(lower_factor, identity, left_side=True, lower...  41.3 us
    all_gather x2, blocking collectives, all_blocks(): pieces = lax.all_gather(pieces, axes[k], axis=0, tiled=True)  21.9 us
    all_gather x1, waiting for transfers between devices, local(): lax.all_gather(ortho_half, ROW, axis=0, tiled=True)  15.3 us
  transfers between devices with their start and end apart: 5, of which 4 were waited for; matrix products, arithmetic and copies ran while one was open for 1% of the time, Pallas kernels for 0%

commit v1 on v0

v1 whole, which is shorter than its diff:
```python
import math

import jax
import jax.numpy as jnp
from jax import lax
from jax.experimental import pallas as pl
from jax.experimental.pallas import tpu as pltpu
from jax.sharding import Mesh
from jax.sharding import PartitionSpec as P

ROWS = 3584
FF = 2048
RANK = 512
X, Z, Y, C = "expert_0", "expert_1", "row_0", "row_1"
ROW = (Y, C)
EXPERT = (X, Z)
NX, NZ, NY, NC = 4, 8, 8, 2
MINE = ROWS // (NY * NC)
SLAB = FF // (NY * NC)
TILE = 128
TILES = RANK // TILE
PAIRS = [(i, j) for i in range(TILES) for j in range(i, TILES)]
PACKED = len(PAIRS) * TILE
HALF = PACKED // NC
PIECE = HALF // NY

EPS = 1e-06
MU_DECAY = 0.9
CLIP_TARGET = 0.5
GAIN = math.sqrt(ROWS * FF / RANK)

F32 = jnp.float32
BF16 = jnp.bfloat16
HIGHEST = lax.Precision.HIGHEST
MESH = pl.DeviceIdType.MESH


def dot(a, b, ca=1, cb=0, precision=None):
    return lax.dot_general(
        a, b, (((ca,), (cb,)), ((), ())), precision=precision, preferred_element_type=F32
    )


def split(value):
    high = value.astype(BF16)
    return high, (value - high.astype(F32)).astype(BF16)


def send(src, dst, send_sem, recv_sem, **device):
    return pltpu.make_async_remote_copy(
        src_ref=src,
        dst_ref=dst,
        send_sem=send_sem,
        recv_sem=recv_sem,
        device_id=device,
        device_id_type=MESH,
    )


def tile_inverse(z, hook):
    lane = lax.broadcasted_iota(jnp.int32, (1, TILE), 1)
    sub = lax.broadcasted_iota(jnp.int32, (8, 1), 0)
    full = (8, TILE)
    done = []
    for s in range(TILE // 8):
        lo = 8 * s
        rest = TILE - lo - 8
        top = z[:8]
        cols = [jnp.broadcast_to(top[:, lo + k : lo + k + 1], full) for k in range(8)]
        a = {
            (i, k): jnp.broadcast_to(cols[k][i : i + 1, :], full)
            for k in range(8)
            for i in range(k + 1)
        }
        inside = (lane >= lo) & (lane < lo + 8)
        rows = []
        for i in range(8):
            row = jnp.where(inside, (lane == lo + i).astype(F32), top[i : i + 1, :])
            rows.append(jnp.broadcast_to(row, full))
        u = {}
        rec = []
        for j in range(8):
            rec.append(1.0 / a[j, j])
            for i in range(j + 1, 8):
                u[j, i] = a[j, i] * rec[j]
            for i in range(j + 1, 8):
                for k in range(i, 8):
                    a[i, k] = a[i, k] - u[j, i] * a[j, k]
            for i in range(j + 1, 8):
                rows[i] = rows[i] - u[j, i] * rows[j]
        out = rows[0] * lax.rsqrt(a[0, 0])
        for j in range(1, 8):
            out = jnp.where(sub == j, rows[j] * lax.rsqrt(a[j, j]), out)
        done.append(jnp.where(lane < lo + 8, out, 0.0))
        if rest:
            below = z[8:]
            scaled = [rows[j] * rec[j] for j in range(8)]
            new = []
            for g in range(rest // 8):
                zg = below[8 * g : 8 * g + 8]
                c = [jnp.broadcast_to(zg[:, lo + k : lo + k + 1], full) for k in range(8)]
                for j in range(8):
                    for i in range(j + 1, 8):
                        c[i] = c[i] - c[j] * u[j, i]
                acc = jnp.where(inside, 0.0, zg)
                for j in range(8):
                    acc = acc - c[j] * scaled[j]
                new.append(acc)
            z = jnp.concatenate(new, axis=0) if len(new) > 1 else new[0]
        hook()
    return jnp.concatenate(done, axis=0)


class Gather:
    def __init__(self, buf, half, sems, y, c):
        self.buf, self.half, self.y, self.c = buf, half, y, c
        self.ring_send, self.ring_recv, self.core_send, self.core_recv = sems
        self.sent = []

    def part(self, chip, core, h):
        return self.buf.at[2 * lax.rem(chip, NY) + core, pl.ds(h * self.half, self.half)]

    def origin(self, side, k):
        return self.y + (NY - 1 - k if side == 0 else 1 + k)

    def hop(self, side, k, h, chip):
        ref = self.part(chip, self.c, h)
        i = side * 8 + k * 2 + h
        to = lax.rem(self.y + (1 if side == 0 else NY - 1), NY)
        return send(ref, ref, self.ring_send.at[i], self.ring_recv.at[i], row_0=to)

    def across(self, i, chip, core, h):
        ref = self.part(chip, core, h)
        return send(ref, ref, self.core_send.at[i], self.core_recv.at[i], row_1=1 - self.c)

    def begin(self):
        for h in range(2):
            for side in range(2):
                copy = self.hop(side, 0, h, self.y)
                copy.start()
                self.sent.append(copy)
        for h in range(2):
            copy = self.across(16 + h, self.y, self.c, h)
            copy.start()
            self.sent.append(copy)

    @staticmethod
    def halves(k, side):
        return (0, 1) if k < 3 else (side,)

    def steps(self):
        return [(k, h) for k in range(4) for h in range(2)]

    def step(self, k, h):
        for side in range(2):
            if h not in self.halves(k, side):
                continue
            chip = self.origin(side, k)
            self.hop(side, k, h, chip).wait_recv()
            if k < 3 and h in self.halves(k + 1, side):
                copy = self.hop(side, k + 1, h, chip)
                copy.start()
                self.sent.append(copy)
            copy = self.across(side * 8 + k * 2 + h, chip, self.c, h)
            copy.start()
            self.sent.append(copy)

    def own_across(self):
        for h in range(2):
            self.across(16 + h, self.y, 1 - self.c, h).wait_recv()

    def far_across(self, k):
        for h in range(2):
            for side in range(2):
                if h in self.halves(k, side):
                    chip = self.origin(side, k)
                    self.across(side * 8 + k * 2 + h, chip, 1 - self.c, h).wait_recv()

    def drain(self):
        for copy in self.sent:
            copy.wait_send()


def kernel(
    mom_hbm,
    grad_hbm,
    basis_ref,
    ranks_ref,
    assign_ref,
    nm_hbm,
    up_hbm,
    nb_ref,
    mom,
    grad,
    full,
    buf,
    ball,
    power,
    packed,
    gtx,
    grx,
    gsum,
    gpieces,
    gall,
    tpart,
    ttx,
    trx,
    rtx,
    rrx,
    tall,
    amat,
    wmat,
    fhalf,
    nm,
    up,
    ps_tx,
    ps_rx,
    load_sem,
    out_sem,
    ps_send,
    ps_recv,
    b_ring_send,
    b_ring_recv,
    b_core_send,
    b_core_recv,
    t_ring_send,
    t_ring_recv,
    t_core_send,
    t_core_recv,
    g_send,
    g_recv,
    r_send,
    r_recv,
    x_send,
    x_recv,
):
    x, z, y, c = (lax.axis_index(a) for a in (X, Z, Y, C))
    load_grad = pltpu.make_async_copy(grad_hbm, grad, load_sem.at[0])
    load_mom = pltpu.make_async_copy(mom_hbm, mom, load_sem.at[1])
    load_grad.start()
    load_mom.start()

    peers = [{C: 1 - c}]
    peers += [{Z: lax.rem(z + k, NZ)} for k in range(1, NZ)]
    peers += [{X: lax.rem(x + k, NX)} for k in range(1, NX)]
    peers += [{Y: lax.rem(y + k, NY)} for k in range(1, NY)]
    barrier = pltpu.get_barrier_semaphore()
    for peer in peers:
        pl.semaphore_signal(barrier, inc=1, device_id=peer, device_id_type=MESH)

    rank = ranks_ref[assign_ref[x * NZ + z]]
    col_id = lax.broadcasted_iota(jnp.int32, (1, RANK), 1)
    mine = 2 * y + c
    ball[mine] = jnp.where(col_id < rank, basis_ref[...], 0.0).astype(BF16)
    pl.semaphore_wait(barrier, len(peers))

    gather_b = Gather(ball, SLAB // 2, (b_ring_send, b_ring_recv, b_core_send, b_core_recv), y, c)
    gather_b.begin()

    load_grad.wait()

    def add_squares(i, acc):
        rows = grad[pl.ds(pl.multiple_of(i * 16, 16), 16), :].astype(F32)
        acc = list(acc)
        for t in range(FF // TILE):
            for r in range(2):
                piece = rows[8 * r : 8 * r + 8, t * TILE : (t + 1) * TILE]
                acc[(2 * t + r) % 4] = acc[(2 * t + r) % 4] + piece * piece
        return tuple(acc)

    zero = jnp.zeros((8, TILE), F32)
    acc = lax.fori_loop(0, MINE // 16, add_squares, (zero,) * 4)
    total = (acc[0] + acc[1]) + (acc[2] + acc[3])
    all_sent = []

    def share(stage, base, value, axis, place, size):
        ps_tx[stage] = value
        copies = []
        for k in range(1, size):
            i = base + k - 1
            copy = send(
                ps_tx.at[stage],
                ps_rx.at[i],
                ps_send.at[i],
                ps_recv.at[i],
                **{axis: lax.rem(place + k, size)},
            )
            copy.start()
            copies.append(copy)
        all_sent.extend(copies)
        return copies

    def collect(base, value, copies):
        for k, copy in enumerate(copies):
            copy.wait_recv()
            value = value + ps_rx[base + k]
        return value

    stage_c = share(0, 0, total, C, c, NC)
    total = collect(0, total, stage_c)
    stage_z = share(1, 1, total, Z, z, NZ)
    gather_b.step(0, 0)
    total = collect(1, total, stage_z)
    stage_x = share(2, 8, total, X, x, NX)
    gather_b.step(0, 1)
    total = collect(8, total, stage_x)
    stage_y = share(3, 11, total, Y, y, NY)
    gather_b.step(1, 0)
    gather_b.step(1, 1)
    total = collect(11, total, stage_y)
    mean_sq = jnp.sum(total, keepdims=True) / float(NX * NZ * ROWS * FF)
    clip = jnp.minimum(1.0, CLIP_TARGET * lax.rsqrt(mean_sq + EPS))

    load_mom.wait()
    for i in range(MINE // 32):
        at = pl.ds(i * 32, 32)
        value = mom[at, :].astype(F32) + clip * grad[at, :].astype(F32)
        full[at, :] = value
        buf[at, :] = value.astype(BF16)
    gather_b.step(2, 0)
    gather_b.step(2, 1)

    def times_chip(chip):
        chip = lax.rem(chip, NY)
        cols = pl.ds(pl.multiple_of(chip * 2 * SLAB, 2 * SLAB), 2 * SLAB)
        basis = ball[pl.ds(2 * chip, 2)].reshape(2 * SLAB, RANK)
        return dot(buf[:, cols], basis)

    gather_b.own_across()
    power[...] = times_chip(y)
    for k in range(3):
        gather_b.far_across(k)
        power[...] = power[...] + (times_chip(y + NY - 1 - k) + times_chip(y + 1 + k))
    gather_b.step(3, 0)
    gather_b.step(3, 1)
    gather_b.far_across(3)
    pw = power[...] + times_chip(y + 4)
    power[...] = pw

    turned = pw.T
    pt_hi, pt_lo = split(turned)
    p_hi, p_lo = split(pw)
    at = 0
    for i in range(TILES):
        r = slice(i * TILE, (i + 1) * TILE)
        strip = (
            dot(pt_hi[r], p_hi[:, i * TILE :])
            + dot(pt_hi[r], p_lo[:, i * TILE :])
            + dot(pt_lo[r], p_hi[:, i * TILE :])
        )
        for j in range(TILES - i):
            packed[at : at + TILE, :] = strip[:, j * TILE : (j + 1) * TILE]
            at += TILE
    other = pl.ds(pl.multiple_of((1 - c) * HALF, HALF), HALF)
    own_half = pl.ds(pl.multiple_of(c * HALF, HALF), HALF)
    gtx[...] = packed[other, :].astype(BF16)
    g_across = send(gtx, grx, g_send.at[0], g_recv.at[0], row_1=1 - c)
    g_across.start()
    all_sent.append(g_across)

    for chip in range(NY):
        part = dot(pt_hi, buf[:, chip * 2 * SLAB : (chip + 1) * 2 * SLAB])
        tpart[0, chip] = part[:, :SLAB]
        tpart[1, chip] = part[:, SLAB:]
    for chip in range(NY):
        ttx[chip] = tpart[1 - c, chip].astype(BF16)
    t_across = send(ttx, trx, x_send.at[0], x_recv.at[0], row_1=1 - c)

    g_across.wait_recv()
    gsum[...] = packed[own_half, :] + grx[...].astype(F32)
    for k in range(NY):
        gpieces[NY + k] = gsum[pl.ds(k * PIECE, PIECE), :].astype(BF16)
    copies = []
    for k in range(1, NY):
        to = lax.rem(y + k, NY)
        copy = send(
            gpieces.at[NY + to], gpieces.at[k], g_send.at[k], g_recv.at[k], row_0=to
        )
        copy.start()
        copies.append(copy)
    t_across.start()
    all_sent.extend(copies)
    all_sent.append(t_across)
    own_piece = gsum[pl.ds(pl.multiple_of(y * PIECE, PIECE), PIECE), :]
    for k, copy in enumerate(copies):
        copy.wait_recv()
        own_piece = own_piece + gpieces[k + 1].astype(F32)
    here = pl.ds(pl.multiple_of(c * HALF + y * PIECE, PIECE), PIECE)
    gall[here, :] = own_piece.astype(BF16)
    copies = []
    for k in range(1, NY):
        copy = send(
            gall.at[here],
            gall.at[here],
            g_send.at[NY + k],
            g_recv.at[NY + k],
            row_0=lax.rem(y + k, NY),
        )
        copy.start()
        copies.append(copy)
    all_sent.extend(copies)

    quarter = RANK // 2

    def both(chip):
        chip = lax.rem(chip, NY)
        return tpart[c, chip] + trx[chip].astype(F32)

    def ring(side, i, h):
        at = pl.ds(h * quarter, quarter)
        n = side * 8 + i * 2 + h
        to = lax.rem(y + (1 if side == 0 else NY - 1), NY)
        return send(
            rtx.at[side * 4 + i, at], rrx.at[side * 4 + i, at], r_send.at[n], r_recv.at[n], row_0=to
        )

    def reduce_step(i, h):
        for side in range(2):
            if i == 0 and h != side:
                continue
            chip = lax.rem(y + (4 - i if side == 0 else NY - 4 + i), NY)
            at = pl.ds(h * quarter, quarter)
            value = tpart[c, chip, at] + trx[chip, at].astype(F32)
            if i > 1 or (i == 1 and h == side):
                ring(side, i - 1, h).wait_recv()
                value = value + rrx[side * 4 + i - 1, at].astype(F32)
            rtx[side * 4 + i, at] = value.astype(BF16)
            copy = ring(side, i, h)
            copy.start()
            all_sent.append(copy)

    gather_t = Gather(tall, quarter, (t_ring_send, t_ring_recv, t_core_send, t_core_recv), y, c)

    def reduce_first():
        t_across.wait_recv()
        reduce_step(0, 0)
        reduce_step(0, 1)

    def reduce_last():
        for h in range(2):
            at = pl.ds(h * quarter, quarter)
            value = tpart[c, y, at] + trx[y, at].astype(F32)
            for side in range(2):
                ring(side, 3, h).wait_recv()
                value = value + rrx[side * 4 + 3, at].astype(F32)
            tall[mine, at] = value.astype(BF16)
        gather_t.begin()

    def job(fn, *args):
        return lambda: fn(*args)

    jobs = [reduce_first]
    for i in range(1, 4):
        jobs += [job(reduce_step, i, h) for h in range(2)]
    jobs += [reduce_last]
    jobs += [job(gather_t.step, k, h) for k, h in gather_t.steps()]

    jobs.pop(0)()
    for copy in copies:
        copy.wait_recv()
    g_half = send(gall.at[own_half], gall.at[own_half], g_send.at[8], g_recv.at[8], row_1=1 - c)
    g_half.start()
    all_sent.append(g_half)
    send(gall.at[other], gall.at[other], g_send.at[8], g_recv.at[8], row_1=1 - c).wait_recv()

    row_id = lax.broadcasted_iota(jnp.int32, (TILE, 1), 0)
    lane_id = lax.broadcasted_iota(jnp.int32, (1, TILE), 1)
    for n, (i, j) in enumerate(PAIRS):
        r, l = row_id + i * TILE, lane_id + j * TILE
        value = gall[n * TILE : (n + 1) * TILE, :].astype(F32)
        value = jnp.where((r < rank) & (l < rank), value, 0.0)
        if i == j:
            value = value + jnp.where((r == l) & (r >= rank), 1.0, 0.0)
        amat[i * TILE : (i + 1) * TILE, j * TILE : (j + 1) * TILE] = value
    wmat[...] = jnp.zeros_like(wmat)

    ticks = [0]

    def hook():
        ticks[0] += 1
        if ticks[0] % 4 == 0 and jobs:
            jobs.pop(0)()

    for b in range(TILES):
        lo, hi = b * TILE, (b + 1) * TILE
        inv = tile_inverse(amat[lo:hi, lo:hi], hook)
        if b:
            wmat[lo:hi, :lo] = dot(inv, wmat[lo:hi, :lo], precision=HIGHEST)
        wmat[lo:hi, lo:hi] = inv
        if b < TILES - 1:
            strip = dot(inv, amat[lo:hi, hi:], precision=HIGHEST)
            amat[hi:, hi:] = amat[hi:, hi:] - dot(strip, strip, 0, 0, HIGHEST)
            wmat[hi:, :hi] = wmat[hi:, :hi] - dot(strip, wmat[lo:hi, :hi], 0, 0, HIGHEST)
    while jobs:
        jobs.pop(0)()

    w_hi, w_lo = split(wmat[...])
    pw = power[...]
    p_hi, p_lo = split(pw)
    ortho = dot(p_hi, w_hi, 1, 1) + dot(p_lo, w_hi, 1, 1) + dot(p_hi, w_lo, 1, 1)
    ortho_half = ortho.astype(BF16)
    gather_t.own_across()
    for k in range(4):
        gather_t.far_across(k)
    outs = []
    squares = jnp.zeros((RANK, TILE), F32)
    mid = RANK // 2
    wide = 2 * SLAB
    for chip in range(NY):
        cols = slice(chip * wide, (chip + 1) * wide)
        t = jnp.concatenate([tall[2 * chip], tall[2 * chip + 1]], axis=1)
        upper = dot(w_hi[:mid, :mid], t[:mid]) + dot(w_lo[:mid, :mid], t[:mid])
        lower = dot(w_hi[mid:], t) + dot(w_lo[mid:], t)
        fac = jnp.concatenate([upper, lower], axis=0)
        squares = squares + (fac[:, :TILE] * fac[:, :TILE] + fac[:, TILE:] * fac[:, TILE:])
        fh = fac.astype(BF16)
        fhalf[chip] = fh
        back = dot(ortho_half, fh)
        nm[:, cols] = (full[:, cols] - (1.0 - MU_DECAY) * back).astype(BF16)
        copy = pltpu.make_async_copy(nm.at[:, cols], nm_hbm.at[:, cols], out_sem.at[chip])
        copy.start()
        outs.append(copy)
    t = tall[mine]
    own_fac = dot(t, w_hi, 0, 1) + dot(t, w_lo, 0, 1)
    col_sq = jnp.sum(squares, axis=1, keepdims=True)
    inv_col = lax.rsqrt(col_sq + EPS)
    inv_norm = jnp.broadcast_to(inv_col, (RANK, TILE)).T[:1, :]
    nb_ref[...] = own_fac * inv_norm
    scaled = (ortho * (inv_norm * GAIN)).astype(BF16)
    for chip in range(NY):
        cols = slice(chip * wide, (chip + 1) * wide)
        up[:, cols] = dot(scaled, fhalf[chip]).astype(BF16)
        copy = pltpu.make_async_copy(up.at[:, cols], up_hbm.at[:, cols], out_sem.at[NY + chip])
        copy.start()
        outs.append(copy)
    for copy in all_sent:
        copy.wait_send()
    gather_b.drain()
    gather_t.drain()
    for copy in outs:
        copy.wait()


def local(momentum, gradient, basis, ranks, assignment):
    any_space = pl.BlockSpec(memory_space=pl.ANY)
    vmem = pl.BlockSpec(memory_space=pltpu.VMEM)
    smem = pl.BlockSpec(memory_space=pltpu.SMEM)
    dma = pltpu.SemaphoreType.DMA
    outs = pl.pallas_call(
        kernel,
        out_shape=(
            jax.ShapeDtypeStruct((MINE, FF), BF16),
            jax.ShapeDtypeStruct((MINE, FF), BF16),
            jax.ShapeDtypeStruct((SLAB, RANK), F32),
        ),
        in_specs=[any_space, any_space, vmem, smem, smem],
        out_specs=(any_space, any_space, vmem),
        scratch_shapes=[
            pltpu.VMEM((MINE, FF), BF16),
            pltpu.VMEM((MINE, FF), BF16),
            pltpu.VMEM((MINE, FF), F32),
            pltpu.VMEM((MINE, FF), BF16),
            pltpu.VMEM((16, SLAB, RANK), BF16),
            pltpu.VMEM((MINE, RANK), F32),
            pltpu.VMEM((PACKED, TILE), F32),
            pltpu.VMEM((HALF, TILE), BF16),
            pltpu.VMEM((HALF, TILE), BF16),
            pltpu.VMEM((HALF, TILE), F32),
            pltpu.VMEM((2 * NY, PIECE, TILE), BF16),
            pltpu.VMEM((PACKED, TILE), BF16),
            pltpu.VMEM((2, NY, RANK, SLAB), F32),
            pltpu.VMEM((NY, RANK, SLAB), BF16),
            pltpu.VMEM((NY, RANK, SLAB), BF16),
            pltpu.VMEM((8, RANK, SLAB), BF16),
            pltpu.VMEM((8, RANK, SLAB), BF16),
            pltpu.VMEM((16, RANK, SLAB), BF16),
            pltpu.VMEM((RANK, RANK), F32),
            pltpu.VMEM((RANK, RANK), F32),
            pltpu.VMEM((NY, RANK, 2 * SLAB), BF16),
            pltpu.VMEM((MINE, FF), BF16),
            pltpu.VMEM((MINE, FF), BF16),
            pltpu.VMEM((4, 8, TILE), F32),
            pltpu.VMEM((18, 8, TILE), F32),
            dma((2,)),
            dma((16,)),
            dma((18,)),
            dma((18,)),
            dma((16,)),
            dma((16,)),
            dma((18,)),
            dma((18,)),
            dma((16,)),
            dma((16,)),
            dma((18,)),
            dma((18,)),
            dma((16,)),
            dma((16,)),
            dma((16,)),
            dma((16,)),
            dma((1,)),
            dma((1,)),
        ],
        compiler_params=pltpu.CompilerParams(
            collective_id=0, has_side_effects=True, vmem_limit_bytes=52 << 20
        ),
        cost_estimate=pl.CostEstimate(
            flops=4 << 30, bytes_accessed=5 << 20, transcendentals=0
        ),
    )(momentum[0], gradient[0], basis[0], ranks, assignment)
    return tuple(o[None] for o in outs)


def solution(mesh):
    torus = Mesh(mesh.devices.reshape(NX, NZ, NY, NC), (X, Z, Y, C))
    return jax.shard_map(
        local,
        mesh=torus,
        in_specs=(P(EXPERT, ROW, None), P(EXPERT, ROW, None), P(EXPERT, ROW, None), P(), P()),
        out_specs=(P(EXPERT, ROW, None), P(EXPERT, ROW, None), P(EXPERT, ROW, None)),
        check_vma=False,
    )
```

time: 426 us -> 105 us (0.25)
  other arithmetic: 134 us -> 0 us
  blocking collectives: 125 us -> 0 us
  waiting for transfers between devices: 106 us -> 0 us
  Pallas kernels: 0 us -> 98.6 us
  matrix products: 22.8 us -> 0 us
  between operations: 17.7 us -> 0.67 us
  local copies, waits for them, and re-layouts: 17.2 us -> 4.73 us
    another operation x17 -> x0, other arithmetic: 120 us -> none  [the longest x14 78.7 us: local(): lower_factor = jnp.linalg.cholesky(gram_sum)]
    pallas_call x0 -> x1, Pallas kernels: none -> 98.6 us  [local(): pl.pallas_call(kernel, out_shape=(jax.ShapeDtypeStruct((MINE, FF), BF16),...]
    all_gather x3 -> x0, waiting for transfers between devices: 56.9 us -> none  [the longest x1 41.6 us: local(): lax.all_gather(factor.astype(jnp.bfloat16), ROW, axis=0, tiled=True)]
    psum x4 -> x0, blocking collectives: 50.9 us -> none  [by_axis(): value = lax.psum(value, axis)]
    reduce_scatter x2 -> x0, waiting for transfers between devices: 48.7 us -> none  [reduced_to_own(): pieces = lax.psum_scatter(pieces, axes[k], scatter_dimension=0, tiled=True)]
    all_to_all x1 -> x0, blocking collectives: 43.9 us -> none  [local(): lax.all_to_all(buffer, ROW, split_axis=1, concat_axis=0, tiled=True)]
    all_gather x3 -> x0, blocking collectives: 30.6 us -> none  [the longest x2 21.9 us: all_blocks(): pieces = lax.all_gather(pieces, axes[k], axis=0, tiled=True)]
    another operation x34 -> x0, local copies, waits for them, and re-layouts: 15.1 us -> none
  transfers between devices with their start and end apart: 5 -> 0, of which waited for: 4 -> 0; matrix products, arithmetic and copies ran while one was open for 1% -> 0% of each run, Pallas kernels for 0% -> 0%
where the time goes in v1:
time: 105 us; the launch traced here: 104 us
  Pallas kernels  98.6 us (94%)
  local copies, waits for them, and re-layouts  4.73 us (5%)
    pallas_call x1, Pallas kernels, local(): pl.pallas_call(kernel, out_shape=(jax.ShapeDtypeStruct((MINE, FF), BF16),...  98.6 us
    unnamed x11, local copies, waits for them, and re-layouts  4.73 us

profile of v1, /device:TPU:1, one launch (start us, length us, event | category | flops | bytes accessed | tf_op | source)
XLA Modules:
  0.0 104.0 jit_solution(6216052937494775175)
XLA Ops:
  0.6 0.0 copy-start.1
  0.6 0.0 copy-start.2
  0.7 0.6 copy-done.1
  1.3 0.0 copy-done.2
  1.3 0.0 copy-start
  1.3 0.9 copy-done
  2.3 98.6 %shard_map.76 = (bf16[224,2048]{1,0:T(8,128)(2,1)S(1)}, bf16[224,2048]{1,0:T(8,128)(2,1)}, f32[128,512]{1,0:T(8,128)S(1)}) custom-call(bf16[224,2048]{1,0:T(8,128)(2,1)} %bitcast.10, bf16[224,2048]{1,0:T(8,128)(2,1)} %bitcast.11, f32[128,512]{1,0:T(8,128)S(1)} %bitcast.8, s32[32]{0:T(128)S(1)} %copy-done.1, s32[32]{0:T(128)S(1)} %copy-done.2), custom_call_target="tpu_custom_call" | custom-call | flops 4294967296 | bytes 5242880 | tf_op jit(solution)/shard_map/pallas_call | solution.py:549
  100.9 0.0 copy-start.3
  100.9 0.9 copy.11
  101.8 0.6 copy-done.3
  102.4 0.9 copy.12
  103.3 0.7 copy.13
Async XLA Ops:
  0.6 0.7 copy-start.1
  0.6 0.7 copy-start.2
  1.3 0.9 copy-start
  100.9 1.5 %copy-start.3 = (bf16[224,2048]{1,0:T(8,128)(2,1)S(1)}, bf16[224,2048]{1,0:T(8,128)(2,1)}, u32[]{:S(2)}) copy-start(bf16[224,2048]{1,0:T(8,128)(2,1)} %get-tuple-element.7) | copy-start | bytes 2752516

commit v2 on v1

v2 whole, which is shorter than its diff:
```python
import math

import jax
import jax.numpy as jnp
from jax import lax
from jax.experimental import pallas as pl
from jax.experimental.pallas import tpu as pltpu
from jax.sharding import Mesh
from jax.sharding import PartitionSpec as P

ROWS = 3584
FF = 2048
RANK = 512
X, Z, Y, C = "expert_0", "expert_1", "row_0", "row_1"
ROW = (Y, C)
EXPERT = (X, Z)
NX, NZ, NY, NC = 4, 8, 8, 2
MINE = ROWS // (NY * NC)
SLAB = FF // (NY * NC)
TILE = 128
TILES = RANK // TILE
PAIRS = [(i, j) for i in range(TILES) for j in range(i, TILES)]
PACKED = len(PAIRS) * TILE
EARLY = 2 * TILE
LATE = PACKED - EARLY
PARTS = 4
ORDER = ((2, 3, 0, 1), (0, 1, 2, 3))

EPS = 1e-06
MU_DECAY = 0.9
CLIP_TARGET = 0.5
GAIN = math.sqrt(ROWS * FF / RANK)

T_PLAN = (2, 6, 19, 31, 11, 2)

F32 = jnp.float32
BF16 = jnp.bfloat16
HIGHEST = lax.Precision.HIGHEST
MESH = pl.DeviceIdType.MESH


def dot(a, b, ca=1, cb=0, precision=None):
    return lax.dot_general(
        a, b, (((ca,), (cb,)), ((), ())), precision=precision, preferred_element_type=F32
    )


def split(value):
    high = value.astype(BF16)
    return high, (value - high.astype(F32)).astype(BF16)


def send(src, dst, send_sem, recv_sem, **device):
    return pltpu.make_async_remote_copy(
        src_ref=src,
        dst_ref=dst,
        send_sem=send_sem,
        recv_sem=recv_sem,
        device_id=device,
        device_id_type=MESH,
    )


def tile_inverse(z, hook):
    lane = lax.broadcasted_iota(jnp.int32, (1, TILE), 1)
    sub = lax.broadcasted_iota(jnp.int32, (8, 1), 0)
    full = (8, TILE)
    done = []
    for s in range(TILE // 8):
        lo = 8 * s
        rest = TILE - lo - 8
        top = z[:8]
        cols = [jnp.broadcast_to(top[:, lo + k : lo + k + 1], full) for k in range(8)]
        a = {
            (i, k): jnp.broadcast_to(cols[k][i : i + 1, :], full)
            for k in range(8)
            for i in range(k + 1)
        }
        inside = (lane >= lo) & (lane < lo + 8)
        rows = []
        for i in range(8):
            row = jnp.where(inside, (lane == lo + i).astype(F32), top[i : i + 1, :])
            rows.append(jnp.broadcast_to(row, full))
        u = {}
        rec = []
        for j in range(8):
            rec.append(1.0 / a[j, j])
            for i in range(j + 1, 8):
                u[j, i] = a[j, i] * rec[j]
            for i in range(j + 1, 8):
                for k in range(i, 8):
                    a[i, k] = a[i, k] - u[j, i] * a[j, k]
            for i in range(j + 1, 8):
                rows[i] = rows[i] - u[j, i] * rows[j]
        out = rows[0] * lax.rsqrt(a[0, 0])
        for j in range(1, 8):
            out = jnp.where(sub == j, rows[j] * lax.rsqrt(a[j, j]), out)
        done.append(jnp.where(lane < lo + 8, out, 0.0))
        if rest:
            below = z[8:]
            scaled = [rows[j] * rec[j] for j in range(8)]
            new = []
            for g in range(rest // 8):
                zg = below[8 * g : 8 * g + 8]
                c = [jnp.broadcast_to(zg[:, lo + k : lo + k + 1], full) for k in range(8)]
                for j in range(8):
                    for i in range(j + 1, 8):
                        c[i] = c[i] - c[j] * u[j, i]
                acc = jnp.where(inside, 0.0, zg)
                for j in range(8):
                    acc = acc - c[j] * scaled[j]
                new.append(acc)
            z = jnp.concatenate(new, axis=0) if len(new) > 1 else new[0]
        hook()
    return jnp.concatenate(done, axis=0)


class Gather:
    def __init__(self, buf, rows, sems, y, c):
        self.buf, self.rows, self.y, self.c = buf, rows, y, c
        self.ring_send, self.ring_recv, self.core_send, self.core_recv = sems
        self.sent = []

    def part(self, chip, core, h):
        return self.buf.at[2 * lax.rem(chip, NY) + core, pl.ds(h * self.rows, self.rows)]

    def origin(self, side, k):
        return self.y + (NY - 1 - k if side == 0 else 1 + k)

    @staticmethod
    def index(side, k, h):
        return (side * 4 + k) * PARTS + h

    def hop(self, side, k, h, chip):
        ref = self.part(chip, self.c, h)
        i = self.index(side, k, h)
        to = lax.rem(self.y + (1 if side == 0 else NY - 1), NY)
        return send(ref, ref, self.ring_send.at[i], self.ring_recv.at[i], row_0=to)

    def across(self, i, chip, core, h):
        ref = self.part(chip, core, h)
        return send(ref, ref, self.core_send.at[i], self.core_recv.at[i], row_1=1 - self.c)

    def go(self, copy):
        copy.start()
        self.sent.append(copy)

    def begin(self):
        for q in range(PARTS):
            for side in range(2):
                self.go(self.hop(side, 0, ORDER[side][q], self.y))
        for h in range(PARTS):
            self.go(self.across(8 * PARTS + h, self.y, self.c, h))

    @staticmethod
    def pieces(k, side):
        return ORDER[side] if k < 3 else ORDER[side][: PARTS // 2]

    def step(self, k, q):
        for side in range(2):
            if q >= len(self.pieces(k, side)):
                continue
            h = ORDER[side][q]
            chip = self.origin(side, k)
            self.hop(side, k, h, chip).wait_recv()
            if k < 3 and h in self.pieces(k + 1, side):
                self.go(self.hop(side, k + 1, h, chip))
            self.go(self.across(self.index(side, k, h), chip, self.c, h))

    def own_across(self):
        for h in range(PARTS):
            self.across(8 * PARTS + h, self.y, 1 - self.c, h).wait_recv()

    def far_across(self, k):
        for side in range(2):
            for h in self.pieces(k, side):
                chip = self.origin(side, k)
                self.across(self.index(side, k, h), chip, 1 - self.c, h).wait_recv()

    def drain(self):
        for copy in self.sent:
            copy.wait_send()


class GramSum:
    def __init__(self, base, half, terms, bufs, sems, y, c):
        self.base, self.half, self.piece = base, half, half // NY
        self.terms, self.y, self.c = terms, y, c
        self.tx, self.rx, self.pieces, self.out = bufs
        self.send_sem, self.recv_sem = sems
        self.sent = []

    def go(self, copy):
        copy.start()
        self.sent.append(copy)
        return copy

    def rows(self, core, at=0, size=None):
        start = self.base + core * self.half + at
        size = self.half if size is None else size
        return pl.ds(pl.multiple_of(start, 16), size)

    def to_core(self):
        self.tx[...] = self.terms[self.rows(1 - self.c), :].astype(BF16)
        self.first = self.go(
            send(self.tx, self.rx, self.send_sem.at[0], self.recv_sem.at[0], row_1=1 - self.c)
        )

    def to_owner(self):
        self.first.wait_recv()
        own = self.rows(self.c)
        self.terms[own, :] = self.terms[own, :] + self.rx[...].astype(F32)
        for k in range(NY):
            at = self.rows(self.c, k * self.piece, self.piece)
            self.pieces[NY + k] = self.terms[at, :].astype(BF16)
        self.second = []
        for k in range(1, NY):
            to = lax.rem(self.y + k, NY)
            copy = send(
                self.pieces.at[NY + to],
                self.pieces.at[k],
                self.send_sem.at[k],
                self.recv_sem.at[k],
                row_0=to,
            )
            self.second.append(self.go(copy))

    def to_all(self):
        here = self.rows(self.c, self.y * self.piece, self.piece)
        value = self.terms[here, :]
        for k, copy in enumerate(self.second):
            copy.wait_recv()
            value = value + self.pieces[k + 1].astype(F32)
        self.out[here, :] = value.astype(BF16)
        ref = self.out.at[here]
        self.third = []
        for k in range(1, NY):
            to = lax.rem(self.y + k, NY)
            i = NY + k
            copy = send(ref, ref, self.send_sem.at[i], self.recv_sem.at[i], row_0=to)
            self.third.append(self.go(copy))

    def pass_on(self):
        for copy in self.third:
            copy.wait_recv()
        ref = self.out.at[self.rows(self.c)]
        self.go(send(ref, ref, self.send_sem.at[8], self.recv_sem.at[8], row_1=1 - self.c))

    def finish(self):
        ref = self.out.at[self.rows(1 - self.c)]
        send(ref, ref, self.send_sem.at[8], self.recv_sem.at[8], row_1=1 - self.c).wait_recv()

    def drain(self):
        for copy in self.sent:
            copy.wait_send()


def kernel(
    mom_hbm,
    grad_hbm,
    basis_hbm,
    ranks_hbm,
    assign_hbm,
    nm_hbm,
    up_hbm,
    nb_ref,
    mom,
    grad,
    basis,
    ranks,
    assign,
    full,
    buf,
    ball,
    power,
    packed,
    gtx_a,
    grx_a,
    gpieces_a,
    gtx_b,
    grx_b,
    gpieces_b,
    gall,
    tpart,
    ttx,
    trx,
    rtx,
    rrx,
    tall,
    amat,
    wmat,
    fhalf,
    own_fac,
    nm,
    up,
    ps_tx,
    ps_rx,
    load_sem,
    out_sem,
    ps_send,
    ps_recv,
    b_ring_send,
    b_ring_recv,
    b_core_send,
    b_core_recv,
    t_ring_send,
    t_ring_recv,
    t_core_send,
    t_core_recv,
    ga_send,
    ga_recv,
    gb_send,
    gb_recv,
    r_send,
    r_recv,
    x_send,
    x_recv,
):
    x, z, y, c = (lax.axis_index(a) for a in (X, Z, Y, C))
    load_grad = pltpu.make_async_copy(grad_hbm, grad, load_sem.at[0])
    load_mom = pltpu.make_async_copy(mom_hbm, mom, load_sem.at[1])
    load_basis = pltpu.make_async_copy(basis_hbm, basis, load_sem.at[2])
    load_ranks = pltpu.make_async_copy(ranks_hbm, ranks, load_sem.at[3])
    load_assign = pltpu.make_async_copy(assign_hbm, assign, load_sem.at[4])
    load_ranks.start()
    load_assign.start()
    load_basis.start()
    load_grad.start()
    load_mom.start()

    peers = [{C: 1 - c}]
    peers += [{Z: lax.rem(z + k, NZ)} for k in range(1, NZ)]
    peers += [{X: lax.rem(x + k, NX)} for k in range(1, NX)]
    peers += [{Y: lax.rem(y + k, NY)} for k in range(1, NY)]
    barrier = pltpu.get_barrier_semaphore()
    for peer in peers:
        pl.semaphore_signal(barrier, inc=1, device_id=peer, device_id_type=MESH)

    load_ranks.wait()
    load_assign.wait()
    rank = ranks[assign[x * NZ + z]]
    load_basis.wait()
    col_id = lax.broadcasted_iota(jnp.int32, (1, RANK), 1)
    mine = 2 * y + c
    ball[mine] = jnp.where(col_id < rank, basis[...], 0.0).astype(BF16)
    pl.semaphore_wait(barrier, len(peers))

    gather_b = Gather(ball, SLAB // PARTS, (b_ring_send, b_ring_recv, b_core_send, b_core_recv), y, c)
    gather_b.begin()

    load_grad.wait()

    def add_squares(i, acc):
        rows = grad[pl.ds(pl.multiple_of(i * 16, 16), 16), :].astype(F32)
        acc = list(acc)
        for t in range(FF // TILE):
            for r in range(2):
                piece = rows[8 * r : 8 * r + 8, t * TILE : (t + 1) * TILE]
                acc[(2 * t + r) % 4] = acc[(2 * t + r) % 4] + piece * piece
        return tuple(acc)

    zero = jnp.zeros((8, TILE), F32)
    acc = lax.fori_loop(0, MINE // 16, add_squares, (zero,) * 4)
    total = (acc[0] + acc[1]) + (acc[2] + acc[3])
    all_sent = []

    def share(stage, base, value, axis, place, size):
        ps_tx[stage] = value
        copies = []
        for k in range(1, size):
            i = base + k - 1
            copy = send(
                ps_tx.at[stage],
                ps_rx.at[i],
                ps_send.at[i],
                ps_recv.at[i],
                **{axis: lax.rem(place + k, size)},
            )
            copy.start()
            copies.append(copy)
        all_sent.extend(copies)
        return copies

    def collect(base, value, copies):
        for k, copy in enumerate(copies):
            copy.wait_recv()
            value = value + ps_rx[base + k]
        return value

    stage_c = share(0, 0, total, C, c, NC)
    total = collect(0, total, stage_c)
    stage_z = share(1, 1, total, Z, z, NZ)
    for q in range(PARTS):
        gather_b.step(0, q)
    total = collect(1, total, stage_z)
    stage_x = share(2, 8, total, X, x, NX)
    for q in range(PARTS):
        gather_b.step(1, q)
    total = collect(8, total, stage_x)
    stage_y = share(3, 11, total, Y, y, NY)
    gather_b.step(2, 0)
    gather_b.step(2, 1)
    total = collect(11, total, stage_y)
    gather_b.step(2, 2)
    gather_b.step(2, 3)
    mean_sq = jnp.sum(total, keepdims=True) / float(NX * NZ * ROWS * FF)
    clip = jnp.minimum(1.0, CLIP_TARGET * lax.rsqrt(mean_sq + EPS))

    load_mom.wait()
    for i in range(MINE // 32):
        at = pl.ds(i * 32, 32)
        value = mom[at, :].astype(F32) + clip * grad[at, :].astype(F32)
        full[at, :] = value
        buf[at, :] = value.astype(BF16)

    def times_chip(chip):
        chip = lax.rem(chip, NY)
        cols = pl.ds(pl.multiple_of(chip * 2 * SLAB, 2 * SLAB), 2 * SLAB)
        basis = ball[pl.ds(2 * chip, 2)].reshape(2 * SLAB, RANK)
        return dot(buf[:, cols], basis)

    gather_b.own_across()
    power[...] = times_chip(y)
    for k in range(3):
        gather_b.far_across(k)
        power[...] = power[...] + (times_chip(y + NY - 1 - k) + times_chip(y + 1 + k))
    gather_b.step(3, 0)
    gather_b.step(3, 1)
    gather_b.far_across(3)
    pw = power[...] + times_chip(y + 4)
    power[...] = pw

    turned = pw.T
    pt_hi, pt_lo = split(turned)
    p_hi, p_lo = split(pw)
    at = 0
    for i in range(TILES):
        r = slice(i * TILE, (i + 1) * TILE)
        strip = (
            dot(pt_hi[r], p_hi[:, i * TILE :])
            + dot(pt_hi[r], p_lo[:, i * TILE :])
            + dot(pt_lo[r], p_hi[:, i * TILE :])
        )
        for j in range(TILES - i):
            packed[at : at + TILE, :] = strip[:, j * TILE : (j + 1) * TILE]
            at += TILE
    early = GramSum(
        0, EARLY // 2, packed, (gtx_a, grx_a, gpieces_a, gall), (ga_send, ga_recv), y, c
    )
    late = GramSum(
        EARLY, LATE // 2, packed, (gtx_b, grx_b, gpieces_b, gall), (gb_send, gb_recv), y, c
    )
    early.to_core()
    late.to_core()

    t_across = send(ttx, trx, x_send.at[0], x_recv.at[0], row_1=1 - c)

    def terms(chips):
        for chip in chips:
            part = dot(pt_hi, buf[:, chip * 2 * SLAB : (chip + 1) * 2 * SLAB])
            tpart[0, chip] = part[:, :SLAB]
            tpart[1, chip] = part[:, SLAB:]

    terms(range(0, 2))
    early.to_owner()
    late.to_owner()
    terms(range(2, NY))
    for chip in range(NY):
        ttx[chip] = tpart[1 - c, chip].astype(BF16)
    t_across.start()
    all_sent.append(t_across)

    quarter = RANK // PARTS

    def both(chip, at):
        return tpart[c, chip, at] + trx[chip, at].astype(F32)

    def ring(side, i, h):
        at = pl.ds(h * quarter, quarter)
        n = (side * 4 + i) * PARTS + h
        to = lax.rem(y + (1 if side == 0 else NY - 1), NY)
        return send(
            rtx.at[side * 4 + i, at], rrx.at[side * 4 + i, at], r_send.at[n], r_recv.at[n], row_0=to
        )

    def reduce_step(i, q):
        for side in range(2):
            h = ORDER[side][q]
            chip = lax.rem(y + (4 - i if side == 0 else NY - 4 + i), NY)
            at = pl.ds(h * quarter, quarter)
            value = both(chip, at)
            if i > 1 or (i == 1 and q >= PARTS // 2):
                ring(side, i - 1, h).wait_recv()
                value = value + rrx[side * 4 + i - 1, at].astype(F32)
            rtx[side * 4 + i, at] = value.astype(BF16)
            copy = ring(side, i, h)
            copy.start()
            all_sent.append(copy)

    gather_t = Gather(tall, quarter, (t_ring_send, t_ring_recv, t_core_send, t_core_recv), y, c)

    def reduce_last():
        for h in range(PARTS):
            at = pl.ds(h * quarter, quarter)
            value = both(y, at)
            for side in range(2):
                ring(side, 3, h).wait_recv()
                value = value + rrx[side * 4 + 3, at].astype(F32)
            tall[mine, at] = value.astype(BF16)
        gather_t.begin()

    first, second = (0, 1), (2, 3)
    t_across.wait_recv()
    for q in second:
        reduce_step(0, q)
    early.to_all()
    for q in first:
        reduce_step(1, q)
    late.to_all()
    for q in second:
        reduce_step(1, q)
    early.pass_on()
    for q in first:
        reduce_step(2, q)
    early.finish()

    jobs = {}

    def plan(tick, fn, *args):
        jobs.setdefault(tick, []).append(lambda: fn(*args))

    for n, q in enumerate(second):
        plan(T_PLAN[0] + n, reduce_step, 2, q)
    for q in range(PARTS):
        plan(T_PLAN[1] + 3 * q, reduce_step, 3, q)
    plan(T_PLAN[2], reduce_last)
    for k in range(3):
        for q in range(PARTS):
            plan(T_PLAN[3] + T_PLAN[4] * k + T_PLAN[5] * q, gather_t.step, k, q)

    row_id = lax.broadcasted_iota(jnp.int32, (TILE, 1), 0)
    lane_id = lax.broadcasted_iota(jnp.int32, (1, TILE), 1)
    def unpack(pairs):
        for n, (i, j) in enumerate(PAIRS):
            if n not in pairs:
                continue
            r, l = row_id + i * TILE, lane_id + j * TILE
            value = gall[n * TILE : (n + 1) * TILE, :].astype(F32)
            value = jnp.where((r < rank) & (l < rank), value, 0.0)
            if i == j:
                value = value + jnp.where((r == l) & (r >= rank), 1.0, 0.0)
            amat[i * TILE : (i + 1) * TILE, j * TILE : (j + 1) * TILE] = value

    unpack(range(0, EARLY // TILE))
    wmat[...] = jnp.zeros_like(wmat)

    ticks = [0]

    def hook():
        ticks[0] += 1
        for job in jobs.pop(ticks[0], ()):
            job()

    for b in range(TILES):
        lo, hi = b * TILE, (b + 1) * TILE
        inv = tile_inverse(amat[lo:hi, lo:hi], hook)
        if b == 0:
            late.pass_on()
        if b:
            wmat[lo:hi, :lo] = dot(inv, wmat[lo:hi, :lo], precision=HIGHEST)
        wmat[lo:hi, lo:hi] = inv
        if b == 0:
            late.finish()
            unpack(range(EARLY // TILE, len(PAIRS)))
        if b < TILES - 1:
            strip = dot(inv, amat[lo:hi, hi:], precision=HIGHEST)
            amat[hi:, hi:] = amat[hi:, hi:] - dot(strip, strip, 0, 0, HIGHEST)
            wmat[hi:, :hi] = wmat[hi:, :hi] - dot(strip, wmat[lo:hi, :hi], 0, 0, HIGHEST)
    for tick in sorted(jobs):
        for job in jobs[tick]:
            job()

    w_hi, w_lo = split(wmat[...])
    pw = power[...]
    p_hi, p_lo = split(pw)
    ortho = dot(p_hi, w_hi, 1, 1) + dot(p_lo, w_hi, 1, 1) + dot(p_hi, w_lo, 1, 1)
    ortho_half = ortho.astype(BF16)
    outs = []
    mid = RANK // 2
    wide = 2 * SLAB
    chips = [y]
    for k in range(3):
        chips += [lax.rem(y + NY - 1 - k, NY), lax.rem(y + 1 + k, NY)]
    chips += [lax.rem(y + 4, NY)]
    columns = [pl.ds(pl.multiple_of(chip * wide, wide), wide) for chip in chips]

    def by_chip(n):
        chip, cols = chips[n], columns[n]
        t = jnp.concatenate([tall[2 * chip], tall[2 * chip + 1]], axis=1)
        upper = dot(w_hi[:mid, :mid], t[:mid]) + dot(w_lo[:mid, :mid], t[:mid])
        lower = dot(w_hi[mid:], t) + dot(w_lo[mid:], t)
        fac = jnp.concatenate([upper, lower], axis=0)
        if n == 0:
            own_fac[...] = jnp.where(c == 0, fac[:, :TILE], fac[:, TILE:])
        fh = fac.astype(BF16)
        fhalf[n] = fh
        back = dot(ortho_half, fh)
        nm[:, cols] = (full[:, cols] - (1.0 - MU_DECAY) * back).astype(BF16)
        copy = pltpu.make_async_copy(nm.at[:, cols], nm_hbm.at[:, cols], out_sem.at[n])
        copy.start()
        outs.append(copy)
        return fac[:, :TILE] * fac[:, :TILE] + fac[:, TILE:] * fac[:, TILE:]

    gather_t.own_across()
    squares = by_chip(0)
    for k in range(3):
        if k == 1:
            gather_t.step(3, 0)
            gather_t.step(3, 1)
        gather_t.far_across(k)
        squares = squares + by_chip(2 * k + 1)
        squares = squares + by_chip(2 * k + 2)
    gather_t.far_across(3)
    squares = squares + by_chip(7)
    col_sq = jnp.sum(squares, axis=1, keepdims=True)
    inv_col = lax.rsqrt(col_sq + EPS)
    inv_norm = jnp.broadcast_to(inv_col, (RANK, TILE)).T[:1, :]
    scaled = (ortho * (inv_norm * GAIN)).astype(BF16)
    for n in range(NY):
        cols = columns[n]
        up[:, cols] = dot(scaled, fhalf[n]).astype(BF16)
        copy = pltpu.make_async_copy(up.at[:, cols], up_hbm.at[:, cols], out_sem.at[NY + n])
        copy.start()
        outs.append(copy)
    nb_ref[...] = own_fac[...].T * inv_norm
    for copy in all_sent:
        copy.wait_send()
    for group in (gather_b, gather_t, early, late):
        group.drain()
    for copy in outs:
        copy.wait()


def local(momentum, gradient, basis, ranks, assignment):
    any_space = pl.BlockSpec(memory_space=pl.ANY)
    vmem = pl.BlockSpec(memory_space=pltpu.VMEM)
    dma = pltpu.SemaphoreType.DMA
    outs = pl.pallas_call(
        kernel,
        out_shape=(
            jax.ShapeDtypeStruct((MINE, FF), BF16),
            jax.ShapeDtypeStruct((MINE, FF), BF16),
            jax.ShapeDtypeStruct((SLAB, RANK), F32),
        ),
        in_specs=[any_space] * 5,
        out_specs=(any_space, any_space, vmem),
        scratch_shapes=[
            pltpu.VMEM((MINE, FF), BF16),
            pltpu.VMEM((MINE, FF), BF16),
            pltpu.VMEM((SLAB, RANK), F32),
            pltpu.SMEM((NX * NZ,), jnp.int32),
            pltpu.SMEM((NX * NZ,), jnp.int32),
            pltpu.VMEM((MINE, FF), F32),
            pltpu.VMEM((MINE, FF), BF16),
            pltpu.VMEM((16, SLAB, RANK), BF16),
            pltpu.VMEM((MINE, RANK), F32),
            pltpu.VMEM((PACKED, TILE), F32),
            pltpu.VMEM((EARLY // 2, TILE), BF16),
            pltpu.VMEM((EARLY // 2, TILE), BF16),
            pltpu.VMEM((2 * NY, EARLY // 16, TILE), BF16),
            pltpu.VMEM((LATE // 2, TILE), BF16),
            pltpu.VMEM((LATE // 2, TILE), BF16),
            pltpu.VMEM((2 * NY, LATE // 16, TILE), BF16),
            pltpu.VMEM((PACKED, TILE), BF16),
            pltpu.VMEM((2, NY, RANK, SLAB), F32),
            pltpu.VMEM((NY, RANK, SLAB), BF16),
            pltpu.VMEM((NY, RANK, SLAB), BF16),
            pltpu.VMEM((8, RANK, SLAB), BF16),
            pltpu.VMEM((8, RANK, SLAB), BF16),
            pltpu.VMEM((16, RANK, SLAB), BF16),
            pltpu.VMEM((RANK, RANK), F32),
            pltpu.VMEM((RANK, RANK), F32),
            pltpu.VMEM((NY, RANK, 2 * SLAB), BF16),
            pltpu.VMEM((RANK, SLAB), F32),
            pltpu.VMEM((MINE, FF), BF16),
            pltpu.VMEM((MINE, FF), BF16),
            pltpu.VMEM((4, 8, TILE), F32),
            pltpu.VMEM((18, 8, TILE), F32),
            dma((5,)),
            dma((16,)),
            dma((18,)),
            dma((18,)),
            dma((8 * PARTS,)),
            dma((8 * PARTS,)),
            dma((9 * PARTS,)),
            dma((9 * PARTS,)),
            dma((8 * PARTS,)),
            dma((8 * PARTS,)),
            dma((9 * PARTS,)),
            dma((9 * PARTS,)),
            dma((16,)),
            dma((16,)),
            dma((16,)),
            dma((16,)),
            dma((8 * PARTS,)),
            dma((8 * PARTS,)),
            dma((1,)),
            dma((1,)),
        ],
        compiler_params=pltpu.CompilerParams(
            collective_id=0, has_side_effects=True, vmem_limit_bytes=52 << 20
        ),
        cost_estimate=pl.CostEstimate(
            flops=4 << 30, bytes_accessed=5 << 20, transcendentals=0
        ),
    )(momentum[0], gradient[0], basis[0], ranks, assignment)
    return tuple(o[None] for o in outs)


def solution(mesh):
    torus = Mesh(mesh.devices.reshape(NX, NZ, NY, NC), (X, Z, Y, C))
    return jax.shard_map(
        local,
        mesh=torus,
        in_specs=(P(EXPERT, ROW, None), P(EXPERT, ROW, None), P(EXPERT, ROW, None), P(), P()),
        out_specs=(P(EXPERT, ROW, None), P(EXPERT, ROW, None), P(EXPERT, ROW, None)),
        check_vma=False,
    )
```

time: 105 us -> 89.4 us (0.85)
  Pallas kernels: 98.6 us -> 83.8 us
    pallas_call x1, Pallas kernels: 98.6 us -> 83.8 us  [local(): pl.pallas_call(kernel, out_shape=(jax.ShapeDtypeStruct((MINE, FF), BF16),...]
where the time goes in v2:
time: 89.4 us; the launch traced here: 89.2 us
  Pallas kernels  83.8 us (94%)
  local copies, waits for them, and re-layouts  4.73 us (5%)
    pallas_call x1, Pallas kernels, local(): pl.pallas_call(kernel, out_shape=(jax.ShapeDtypeStruct((MINE, FF), BF16),...  83.8 us
    unnamed x11, local copies, waits for them, and re-layouts  4.73 us

profile of v2, /device:TPU:1, one launch (start us, length us, event | category | flops | bytes accessed | tf_op | source)
XLA Modules:
  0.0 89.2 jit_solution(5332047834281673036)
XLA Ops:
  0.6 0.0 copy-start.1
  0.6 0.0 copy-start.2
  0.7 0.6 copy-done.1
  1.3 0.0 copy-done.2
  1.3 0.0 copy-start
  1.3 0.9 %copy-done = f32[1,128,512]{2,1,0:T(8,128)S(1)} copy-done((f32[1,128,512]{2,1,0:T(8,128)S(1)}, f32[1,128,512]{2,1,0:T(8,128)}, u32[]{:S(2)}) %copy-start) | copy-done | bytes 262168
  2.3 83.8 %shard_map.76 = (bf16[224,2048]{1,0:T(8,128)(2,1)S(1)}, bf16[224,2048]{1,0:T(8,128)(2,1)}, f32[128,512]{1,0:T(8,128)S(1)}) custom-call(bf16[224,2048]{1,0:T(8,128)(2,1)} %bitcast.10, bf16[224,2048]{1,0:T(8,128)(2,1)} %bitcast.11, f32[128,512]{1,0:T(8,128)S(1)} %bitcast.8, s32[32]{0:T(128)S(1)} %copy-done.1, s32[32]{0:T(128)S(1)} %copy-done.2), custom_call_target="tpu_custom_call" | custom-call | flops 4294967296 | bytes 5242880 | tf_op jit(solution)/shard_map/pallas_call | solution.py:648
  86.1 0.0 copy-start.3
  86.1 0.9 %copy.11 = bf16[1,224,2048]{2,1,0:T(8,128)(2,1)} copy(bf16[1,224,2048]{2,1,0:T(8,128)(2,1)S(1)} %bitcast.6) | data formatting | bytes 1835008
  87.0 0.6 copy-done.3
  87.6 0.9 %copy.12 = bf16[1,224,2048]{2,1,0:T(8,128)(2,1)} copy(bf16[1,224,2048]{2,1,0:T(8,128)(2,1)S(1)} %bitcast.9) | data formatting | bytes 1835008
  88.5 0.7 copy.13
Async XLA Ops:
  0.6 0.7 copy-start.1
  0.6 0.7 copy-start.2
  1.3 0.9 %copy-start = (f32[1,128,512]{2,1,0:T(8,128)S(1)}, f32[1,128,512]{2,1,0:T(8,128)}, u32[]{:S(2)}) copy-start(f32[1,128,512]{2,1,0:T(8,128)} %param.7) | copy-start | bytes 786436
  86.1 1.5 %copy-start.3 = (bf16[224,2048]{1,0:T(8,128)(2,1)S(1)}, bf16[224,2048]{1,0:T(8,128)(2,1)}, u32[]{:S(2)}) copy-start(bf16[224,2048]{1,0:T(8,128)(2,1)} %get-tuple-element.7) | copy-start | bytes 2752516
